TPU v7x, 512 devices: a whole 4x4x16 slice. The times are simulated.
512 devices in a mesh: coef: 8 (over y, x_lo), grid: 64 (over z, x_hi, core).
Axes of the slice: x: 4 (x_hi: 2, x_lo: 2; x = x_hi * 2 + x_lo), y: 4, z: 16, core: 2. Of those that a mesh axis runs over, the one named last changes fastest.
Arguments:
- basis_values: bfloat16 [40960, 2688], P('grid'), may hold values from -6 to 6
- occ_coef: bfloat16 [40960, 1024], P('grid', 'coef'), may hold values from -0.125 to 0.125
- listed_panels: int32 [64, 21], P('grid'), may hold values from 0 to 319, as said below
- centres: float32 [3, 40960], replicated, may hold values from 0 to 4
- point_weights: float32 [40960], P('grid'), may hold values from 0.25 to 4
Outputs:
- exchange_tiles: float32 [40960, 1024], P('grid', 'coef')
Inputs may be any that keep to these rules, and one draw needn't show every extreme that they name: `listed_panels`: the panels of one batch are distinct; panel p belongs to batch p // 5, and batch b names only panels of batches b - 4 to b + 4.
All inputs are finite; a program needn't handle non-finite values.
Results may differ from a plain program's by a relative error of at most 0.0085.
Values may be sent and summed in bfloat16 or wider, within the bound.
A program may use at most 64 MiB of HBM per device.

v0:
```python
import jax
import jax.numpy as jnp
from jax import lax
from jax.sharding import PartitionSpec as P

ORBITALS = 1024
PANEL_ROWS = 128
PANELS_DEV = 5
REACH = 4
LISTED = 21


def from_behind(block, axis, distance):
    devices = range(lax.axis_size(axis))
    route = [(i - distance, i) for i in devices if i - distance in devices]
    return lax.ppermute(block, axis, route)


def padded(block, sides, width):
    for axis, dim in sides:
        count = lax.axis_size(axis)
        forward = [(i, i + 1) for i in range(count - 1)]
        backward = [(target, source) for source, target in forward]
        low = lax.ppermute(
            lax.slice_in_dim(block, block.shape[dim] - width, None, axis=dim), axis, forward
        )
        high = lax.ppermute(lax.slice_in_dim(block, 0, width, axis=dim), axis, backward)
        block = jnp.concatenate([low, block, high], axis=dim)
    return block


def nearby(panels, offset):
    return from_behind(panels, "grid", -offset)


def send_back(contrib, offset):
    return from_behind(contrib.astype(jnp.bfloat16), "grid", offset).astype(contrib.dtype)


def shards(basis_values, occ_coef, listed_panels, centres, point_weights):
    width = occ_coef.shape[1]
    points = basis_values.shape[0]
    panels = occ_coef.reshape(PANELS_DEV, PANEL_ROWS, width)
    listed = listed_panels[0]
    batch = lax.axis_index("grid")
    pieces = {0: panels}
    for offset in range(-REACH, REACH + 1):
        if offset != 0:
            pieces[offset] = nearby(panels, offset)
    candidates = jnp.concatenate([pieces[offset] for offset in range(-REACH, REACH + 1)], 0)
    chosen = jnp.take(candidates, listed - (batch - REACH) * PANELS_DEV, axis=0)
    field = jnp.dot(
        basis_values, chosen.reshape(LISTED * PANEL_ROWS, width), preferred_element_type=jnp.float32
    ).astype(jnp.bfloat16)
    near = padded(field, (("grid", 0),), points)
    partial_value = lax.dot_general(
        field, near, (((1,), (1,)), ((), ())), preferred_element_type=jnp.float32
    )
    partial_value = partial_value / jnp.sqrt(jnp.float32(ORBITALS))
    density = lax.psum(partial_value.astype(jnp.bfloat16), "coef").astype(jnp.float32)
    anchor = jnp.zeros((), jnp.int32)
    start = batch * points
    padded_centres = jnp.pad(centres, ((0, 0), (points, points)))
    own_centres = lax.dynamic_slice(centres, (anchor, start), (3, points))
    near_centres = lax.dynamic_slice(padded_centres, (anchor, start), (3, 3 * points))
    distance = jnp.zeros((points, 3 * points), jnp.float32)
    for axis in range(3):
        gap = own_centres[axis][:, None] - near_centres[axis][None, :]
        distance = distance + gap * gap
    kernel = 1.0 / jnp.sqrt(distance + 0.25)
    mixed = (kernel * density).astype(jnp.bfloat16)
    exchanged = jnp.dot(mixed, near, preferred_element_type=jnp.float32)
    weighted = (exchanged * point_weights[:, None] / jnp.sqrt(jnp.float32(3 * points))).astype(
        jnp.bfloat16
    )
    tiles = lax.dot_general(
        basis_values, weighted, (((0,), (0,)), ((), ())), preferred_element_type=jnp.float32
    )
    tiles = (tiles / jnp.sqrt(jnp.float32(points))).reshape(LISTED, PANEL_ROWS, width)
    contribs = {}
    for offset in range(-REACH, REACH + 1):
        first_panel = (batch + offset) * PANELS_DEV
        select = (
            listed[None, :] == first_panel + jnp.arange(PANELS_DEV, dtype=jnp.int32)[:, None]
        ).astype(jnp.float32)
        contribs[offset] = jnp.einsum("js,sro->jro", select, tiles)
    total = contribs[0]
    for offset in range(-REACH, REACH + 1):
        if offset != 0:
            total = total + send_back(contribs[offset], offset)
    return total.reshape(PANELS_DEV * PANEL_ROWS, width)


def solution(mesh):
    placed = (P("grid", None), P("grid", "coef"), P("grid", None), P(), P("grid"))
    return jax.shard_map(
        shards, mesh=mesh, in_specs=placed, out_specs=P("grid", "coef"), check_vma=False
    )
```

profile of v0, /device:TPU:388, one launch (start us, length us, event | category | flops | bytes accessed | tf_op | source)
XLA Modules:
  0.0 277.5 jit_solution(35657123346483395)
XLA Ops:
  6.5 3.2 %collective-permute-start = (bf16[5,128,128]{2,1,0:T(8,128)(2,1)}, bf16[5,128,128]{2,1,0:T(8,128)(2,1)}, u32[]{:S(2)}, u32[]{:S(2)}) collective-permute-start(bf16[5,128,128]{2,1,0:T(8,128)(2,1)} %bitcast.62), channel_id=1, source_target_pairs={{0,4},{1,5},{2,6},{3,7},{4,8},{5,9},{6,10},{7,11},{8,12},{9,13},{1... | collective-permute-start | bytes 491528 | tf_op jit(solution)/shard_map/ppermute | solution.py:16
  9.7 2.0 collective-permute-start.1
  11.8 4.9 %collective-permute-start.2 = (bf16[5,128,128]{2,1,0:T(8,128)(2,1)}, bf16[5,128,128]{2,1,0:T(8,128)(2,1)}, u32[]{:S(2)}, u32[]{:S(2)}) collective-permute-start(bf16[5,128,128]{2,1,0:T(8,128)(2,1)} %bitcast.64), channel_id=1, source_target_pairs={{0,2},{1,3},{2,4},{3,5},{4,6},{5,7},{6,8},{7,9},{8,10},{9,11},{10,... | collective-permute-start | bytes 491528 | tf_op jit(solution)/shard_map/ppermute | solution.py:16
  16.7 1.9 collective-permute-start.3
  18.6 5.1 %collective-permute-start.4 = (bf16[5,128,128]{2,1,0:T(8,128)(2,1)}, bf16[5,128,128]{2,1,0:T(8,128)(2,1)}, u32[]{:S(2)}, u32[]{:S(2)}) collective-permute-start(bf16[5,128,128]{2,1,0:T(8,128)(2,1)} %bitcast.66), channel_id=1, source_target_pairs={{1,0},{2,1},{3,2},{4,3},{5,4},{6,5},{7,6},{8,7},{9,8},{10,9},{11,1... | collective-permute-start | bytes 491528 | tf_op jit(solution)/shard_map/ppermute | solution.py:16
  25.2 4.5 %collective-permute-start.5 = (bf16[5,128,128]{2,1,0:T(8,128)(2,1)}, bf16[5,128,128]{2,1,0:T(8,128)(2,1)S(1)}, u32[]{:S(2)}, u32[]{:S(2)}) collective-permute-start(bf16[5,128,128]{2,1,0:T(8,128)(2,1)} %bitcast.67), channel_id=1, source_target_pairs={{2,0},{3,1},{4,2},{5,3},{6,4},{7,5},{8,6},{9,7},{10,8},{11,9},{12,... | collective-permute-start | bytes 491528 | tf_op jit(solution)/shard_map/ppermute | solution.py:16
  29.8 1.6 constant_dynamic-update-slice_fusion.8
  31.3 1.9 collective-permute-start.6
  33.3 1.6 constant_dynamic-update-slice_fusion.7
  34.8 2.9 %collective-permute-start.7 = (bf16[5,128,128]{2,1,0:T(8,128)(2,1)}, bf16[5,128,128]{2,1,0:T(8,128)(2,1)S(1)}, u32[]{:S(2)}, u32[]{:S(2)}) collective-permute-start(bf16[5,128,128]{2,1,0:T(8,128)(2,1)} %bitcast.69), channel_id=1, source_target_pairs={{4,0},{5,1},{6,2},{7,3},{8,4},{9,5},{10,6},{11,7},{12,8},{13,9},{1... | collective-permute-start | bytes 491528 | tf_op jit(solution)/shard_map/ppermute | solution.py:16
  37.8 1.6 constant_dynamic-update-slice_fusion.6
  39.4 1.6 constant_dynamic-update-slice_fusion.5
  40.9 1.6 constant_dynamic-update-slice_fusion.4
  42.5 1.6 constant_dynamic-update-slice_fusion.3
  45.5 0.7 constant_dynamic-update-slice_fusion
  46.2 2.9 %gather_fusion = bf16[21,128,128]{2,1,0:T(8,128)(2,1)} fusion(bf16[45,128,128]{2,1,0:T(8,128)(2,1)} %constant_dynamic-update-slice_fusion, s32[1024]{0:T(1024)S(1)} %pad_clamp_fusion), kind=kCustom, calls=%fused_computation | custom fusion | bytes 1376340 | tf_op jit(solution)/shard_map/jit(_take)/gather | solution.py:51
  49.1 2.4 bitcast_select_fusion
  51.4 1.1 convolution_convert_fusion
  52.6 4.4 %collective-permute-start.8 = (bf16[640,128]{0,1:T(8,128)(2,1)S(1)}, bf16[640,128]{0,1:T(8,128)(2,1)S(1)}, u32[]{:S(2)}, u32[]{:S(2)}) collective-permute-start(bf16[640,128]{0,1:T(8,128)(2,1)S(1)} %bitcast.58), channel_id=1, source_target_pairs={{0,1},{1,2},{2,3},{3,4},{4,5},{5,6},{6,7},{7,8},{8,9},{9,10},{10,1... | collective-permute-start | bytes 491528 | tf_op jit(solution)/shard_map/ppermute | solution.py:24
  57.0 2.9 %collective-permute-start.9 = (bf16[640,128]{0,1:T(8,128)(2,1)S(1)}, bf16[640,128]{0,1:T(8,128)(2,1)S(1)}, u32[]{:S(2)}, u32[]{:S(2)}) collective-permute-start(bf16[640,128]{0,1:T(8,128)(2,1)S(1)} %bitcast.59), channel_id=1, source_target_pairs={{1,0},{2,1},{3,2},{4,3},{5,4},{6,5},{7,6},{8,7},{9,8},{10,9},{11,1... | collective-permute-start | bytes 491528 | tf_op jit(solution)/shard_map/ppermute | solution.py:27
  60.0 1.1 collective-permute-done.8
  61.0 2.3 collective-permute-done.9
  64.0 2.3 multiply_convert_fusion.1
  66.3 0.9 dynamic-slice_reduce_fusion.2
  67.3 1.0 fusion.49
  68.3 135.7 %all-reduce.3.cloned.1.call-done = bf16[640,1920]{1,0:T(8,128)(2,1)} async-done(((bf16[640,1920]{1,0:T(8,128)(2,1)}), bf16[640,1920]{1,0:T(8,128)(2,1)}) %all-reduce.3.cloned.1.call-update) | async-done | bytes 2457616 | tf_op jit(solution)/shard_map/psum | solution.py:60
  204.1 6.0 %fusion = bf16[2688,128]{0,1:T(8,128)(2,1)} fusion(bf16[640,2688]{1,0:T(8,128)(2,1)S(1)} %copy-done, bf16[640,1920]{1,0:T(8,128)(2,1)} %all-reduce.3.cloned.1.call-done, f32[1920]{0:T(1024)S(1)} %get-tuple-element.10, f32[640]{0:T(1024)S(1)} %get-tuple-element.7, f32[1920]{0:T(1024)S(1)} %get-tuple-element.9, f32[640]{0:T(1024)S(1)} %get-tuple-element.6, ...), kind=kOutput, calls=%fused_computation.4 | convolution fusion | flops 772128768 | bytes 7111168 | tf_op jit(solution)/shard_map/dot_general | solution.py:76
  210.1 2.2 copy.15
  212.3 1.8 fusion.20
  214.1 4.5 %collective-permute-start.10 = (bf16[5,128,128]{2,0,1:T(8,128)(2,1)S(1)}, bf16[5,128,128]{2,0,1:T(8,128)(2,1)}, u32[]{:S(2)}, u32[]{:S(2)}) collective-permute-start(bf16[5,128,128]{2,0,1:T(8,128)(2,1)S(1)} %fusion.20), channel_id=1, source_target_pairs={{4,0},{5,1},{6,2},{7,3},{8,4},{9,5},{10,6},{11,7},{12,8},{13,9},{1... | collective-permute-start | bytes 491528 | tf_op jit(solution)/shard_map/ppermute | solution.py:16
  218.6 1.7 fusion.23
  220.3 2.2 collective-permute-start.11
  222.5 1.7 fusion.26
  224.2 2.8 collective-permute-start.12
  227.0 1.4 fusion.29
  228.4 5.4 %collective-permute-start.13 = (bf16[5,128,128]{2,0,1:T(8,128)(2,1)}, bf16[5,128,128]{2,0,1:T(8,128)(2,1)}, u32[]{:S(2)}, u32[]{:S(2)}) collective-permute-start(bf16[5,128,128]{2,0,1:T(8,128)(2,1)} %fusion.29), channel_id=1, source_target_pairs={{1,0},{2,1},{3,2},{4,3},{5,4},{6,5},{7,6},{8,7},{9,8},{10,9},{11,1... | collective-permute-start | bytes 491528 | tf_op jit(solution)/shard_map/ppermute | solution.py:16
  233.8 1.3 fusion.32
  235.1 2.1 collective-permute-start.14
  237.2 1.3 fusion.35
  238.5 1.3 fusion.38
  239.9 1.3 fusion.41
  241.2 5.5 %collective-permute-start.15 = (bf16[5,128,128]{2,0,1:T(8,128)(2,1)}, bf16[5,128,128]{2,0,1:T(8,128)(2,1)}, u32[]{:S(2)}, u32[]{:S(2)}) collective-permute-start(bf16[5,128,128]{2,0,1:T(8,128)(2,1)} %fusion.35), channel_id=1, source_target_pairs={{0,2},{1,3},{2,4},{3,5},{4,6},{5,7},{6,8},{7,9},{8,10},{9,11},{10,... | collective-permute-start | bytes 491528 | tf_op jit(solution)/shard_map/ppermute | solution.py:16
  246.7 5.0 %collective-permute-start.16 = (bf16[5,128,128]{2,0,1:T(8,128)(2,1)}, bf16[5,128,128]{2,0,1:T(8,128)(2,1)}, u32[]{:S(2)}, u32[]{:S(2)}) collective-permute-start(bf16[5,128,128]{2,0,1:T(8,128)(2,1)} %fusion.38), channel_id=1, source_target_pairs={{0,3},{1,4},{2,5},{3,6},{4,7},{5,8},{6,9},{7,10},{8,11},{9,12},{10... | collective-permute-start | bytes 491528 | tf_op jit(solution)/shard_map/ppermute | solution.py:16
  251.7 1.9 collective-permute-start.17
  253.6 7.6 %collective-permute-done.16 = bf16[5,128,128]{2,0,1:T(8,128)(2,1)} collective-permute-done((bf16[5,128,128]{2,0,1:T(8,128)(2,1)}, bf16[5,128,128]{2,0,1:T(8,128)(2,1)}, u32[]{:S(2)}, u32[]{:S(2)}) %collective-permute-start.16) | collective-permute-done | bytes 163872 | tf_op jit(solution)/shard_map/ppermute | solution.py:16
  261.2 6.1 %collective-permute-done.17 = bf16[5,128,128]{2,0,1:T(8,128)(2,1)} collective-permute-done((bf16[5,128,128]{2,0,1:T(8,128)(2,1)}, bf16[5,128,128]{2,0,1:T(8,128)(2,1)}, u32[]{:S(2)}, u32[]{:S(2)}) %collective-permute-start.17) | collective-permute-done | bytes 163872 | tf_op jit(solution)/shard_map/ppermute | solution.py:16
  267.4 2.5 convert_add_fusion
  269.9 0.8 copy.25
  (45 shorter events, 3.5 us)
Async XLA Ops:
  6.5 44.9 %copy-start = (bf16[640,2688]{1,0:T(8,128)(2,1)S(1)}, bf16[640,2688]{1,0:T(8,128)(2,1)}, u32[]{:S(2)}) copy-start(bf16[640,2688]{1,0:T(8,128)(2,1)} %param.5) | copy-start | bytes 10321924
  6.5 197.6 %all-reduce.3.cloned.1.call-start = ((), (), s32[]{:S(2)}) async-start(), calls=%async_computation | async-start | bytes 4915200 | tf_op jit(solution)/shard_map/psum | solution.py:60
  6.5 18.7 %collective-permute-start = (bf16[5,128,128]{2,1,0:T(8,128)(2,1)}, bf16[5,128,128]{2,1,0:T(8,128)(2,1)}, u32[]{:S(2)}, u32[]{:S(2)}) collective-permute-start(bf16[5,128,128]{2,1,0:T(8,128)(2,1)} %bitcast.62), channel_id=1, source_target_pairs={{0,4},{1,5},{2,6},{3,7},{4,8},{5,9},{6,10},{7,11},{8,12},{9,13},{1... | collective-permute-start | bytes 491528 | tf_op jit(solution)/shard_map/ppermute | solution.py:16
  9.7 21.6 %collective-permute-start.1 = (bf16[5,128,128]{2,1,0:T(8,128)(2,1)}, bf16[5,128,128]{2,1,0:T(8,128)(2,1)}, u32[]{:S(2)}, u32[]{:S(2)}) collective-permute-start(bf16[5,128,128]{2,1,0:T(8,128)(2,1)} %bitcast.63), channel_id=1, source_target_pairs={{0,3},{1,4},{2,5},{3,6},{4,7},{5,8},{6,9},{7,10},{8,11},{9,12},{10... | collective-permute-start | bytes 491528 | tf_op jit(solution)/shard_map/ppermute | solution.py:16
  11.8 23.1 %collective-permute-start.2 = (bf16[5,128,128]{2,1,0:T(8,128)(2,1)}, bf16[5,128,128]{2,1,0:T(8,128)(2,1)}, u32[]{:S(2)}, u32[]{:S(2)}) collective-permute-start(bf16[5,128,128]{2,1,0:T(8,128)(2,1)} %bitcast.64), channel_id=1, source_target_pairs={{0,2},{1,3},{2,4},{3,5},{4,6},{5,7},{6,8},{7,9},{8,10},{9,11},{10,... | collective-permute-start | bytes 491528 | tf_op jit(solution)/shard_map/ppermute | solution.py:16
  16.7 22.6 %collective-permute-start.3 = (bf16[5,128,128]{2,1,0:T(8,128)(2,1)}, bf16[5,128,128]{2,1,0:T(8,128)(2,1)}, u32[]{:S(2)}, u32[]{:S(2)}) collective-permute-start(bf16[5,128,128]{2,1,0:T(8,128)(2,1)} %bitcast.65), channel_id=1, source_target_pairs={{0,1},{1,2},{2,3},{3,4},{4,5},{5,6},{6,7},{7,8},{8,9},{9,10},{10,1... | collective-permute-start | bytes 491528 | tf_op jit(solution)/shard_map/ppermute | solution.py:16
  18.6 23.9 %collective-permute-start.4 = (bf16[5,128,128]{2,1,0:T(8,128)(2,1)}, bf16[5,128,128]{2,1,0:T(8,128)(2,1)}, u32[]{:S(2)}, u32[]{:S(2)}) collective-permute-start(bf16[5,128,128]{2,1,0:T(8,128)(2,1)} %bitcast.66), channel_id=1, source_target_pairs={{1,0},{2,1},{3,2},{4,3},{5,4},{6,5},{7,6},{8,7},{9,8},{10,9},{11,1... | collective-permute-start | bytes 491528 | tf_op jit(solution)/shard_map/ppermute | solution.py:16
  25.2 18.9 %collective-permute-start.5 = (bf16[5,128,128]{2,1,0:T(8,128)(2,1)}, bf16[5,128,128]{2,1,0:T(8,128)(2,1)S(1)}, u32[]{:S(2)}, u32[]{:S(2)}) collective-permute-start(bf16[5,128,128]{2,1,0:T(8,128)(2,1)} %bitcast.67), channel_id=1, source_target_pairs={{2,0},{3,1},{4,2},{5,3},{6,4},{7,5},{8,6},{9,7},{10,8},{11,9},{12,... | collective-permute-start | bytes 491528 | tf_op jit(solution)/shard_map/ppermute | solution.py:16
  31.3 13.5 %collective-permute-start.6 = (bf16[5,128,128]{2,1,0:T(8,128)(2,1)}, bf16[5,128,128]{2,1,0:T(8,128)(2,1)S(1)}, u32[]{:S(2)}, u32[]{:S(2)}) collective-permute-start(bf16[5,128,128]{2,1,0:T(8,128)(2,1)} %bitcast.68), channel_id=1, source_target_pairs={{3,0},{4,1},{5,2},{6,3},{7,4},{8,5},{9,6},{10,7},{11,8},{12,9},{13... | collective-permute-start | bytes 491528 | tf_op jit(solution)/shard_map/ppermute | solution.py:16
  34.8 10.6 %collective-permute-start.7 = (bf16[5,128,128]{2,1,0:T(8,128)(2,1)}, bf16[5,128,128]{2,1,0:T(8,128)(2,1)S(1)}, u32[]{:S(2)}, u32[]{:S(2)}) collective-permute-start(bf16[5,128,128]{2,1,0:T(8,128)(2,1)} %bitcast.69), channel_id=1, source_target_pairs={{4,0},{5,1},{6,2},{7,3},{8,4},{9,5},{10,6},{11,7},{12,8},{13,9},{1... | collective-permute-start | bytes 491528 | tf_op jit(solution)/shard_map/ppermute | solution.py:16
  52.6 10.7 %copy-start.2 = (bf16[128,640]{1,0:T(8,128)(2,1)}, bf16[128,640]{1,0:T(8,128)(2,1)S(1)}, u32[]{:S(2)}) copy-start(bf16[128,640]{1,0:T(8,128)(2,1)S(1)} %convolution_convert_fusion) | copy-start | bytes 491524
  52.6 151.5 %copy-start.6 = (f32[640]{0:T(1024)S(1)}, f32[640]{0:T(1024)}, u32[]{:S(2)}) copy-start(f32[640]{0:T(1024)} %param.9) | copy-start | bytes 7684
  52.6 8.4 %collective-permute-start.8 = (bf16[640,128]{0,1:T(8,128)(2,1)S(1)}, bf16[640,128]{0,1:T(8,128)(2,1)S(1)}, u32[]{:S(2)}, u32[]{:S(2)}) collective-permute-start(bf16[640,128]{0,1:T(8,128)(2,1)S(1)} %bitcast.58), channel_id=1, source_target_pairs={{0,1},{1,2},{2,3},{3,4},{4,5},{5,6},{6,7},{7,8},{8,9},{9,10},{10,1... | collective-permute-start | bytes 491528 | tf_op jit(solution)/shard_map/ppermute | solution.py:24
  57.0 6.3 %collective-permute-start.9 = (bf16[640,128]{0,1:T(8,128)(2,1)S(1)}, bf16[640,128]{0,1:T(8,128)(2,1)S(1)}, u32[]{:S(2)}, u32[]{:S(2)}) collective-permute-start(bf16[640,128]{0,1:T(8,128)(2,1)S(1)} %bitcast.59), channel_id=1, source_target_pairs={{1,0},{2,1},{3,2},{4,3},{5,4},{6,5},{7,6},{8,7},{9,8},{10,9},{11,1... | collective-permute-start | bytes 491528 | tf_op jit(solution)/shard_map/ppermute | solution.py:27
  61.0 2.3 copy-start.3
  63.3 0.7 copy-start.4
  204.1 8.2 %copy-start.5 = (s32[1,21]{1,0:T(1,128)S(1)}, s32[1,21]{1,0:T(1,128)}, u32[]{:S(2)}) copy-start(s32[1,21]{1,0:T(1,128)} %param.7) | copy-start | bytes 256
  212.3 14.7 %copy-start.1 = (bf16[2688,128]{1,0:T(8,128)(2,1)S(1)}, bf16[2688,128]{1,0:T(8,128)(2,1)}, u32[]{:S(2)}) copy-start(bf16[2688,128]{1,0:T(8,128)(2,1)} %copy.15) | copy-start | bytes 2064388
  214.1 27.1 %collective-permute-start.10 = (bf16[5,128,128]{2,0,1:T(8,128)(2,1)S(1)}, bf16[5,128,128]{2,0,1:T(8,128)(2,1)}, u32[]{:S(2)}, u32[]{:S(2)}) collective-permute-start(bf16[5,128,128]{2,0,1:T(8,128)(2,1)S(1)} %fusion.20), channel_id=1, source_target_pairs={{4,0},{5,1},{6,2},{7,3},{8,4},{9,5},{10,6},{11,7},{12,8},{13,9},{1... | collective-permute-start | bytes 491528 | tf_op jit(solution)/shard_map/ppermute | solution.py:16
  220.3 26.4 %collective-permute-start.11 = (bf16[5,128,128]{2,0,1:T(8,128)(2,1)S(1)}, bf16[5,128,128]{2,0,1:T(8,128)(2,1)}, u32[]{:S(2)}, u32[]{:S(2)}) collective-permute-start(bf16[5,128,128]{2,0,1:T(8,128)(2,1)S(1)} %fusion.23), channel_id=1, source_target_pairs={{3,0},{4,1},{5,2},{6,3},{7,4},{8,5},{9,6},{10,7},{11,8},{12,9},{13... | collective-permute-start | bytes 491528 | tf_op jit(solution)/shard_map/ppermute | solution.py:16
  224.2 27.4 %collective-permute-start.12 = (bf16[5,128,128]{2,0,1:T(8,128)(2,1)S(1)}, bf16[5,128,128]{2,0,1:T(8,128)(2,1)}, u32[]{:S(2)}, u32[]{:S(2)}) collective-permute-start(bf16[5,128,128]{2,0,1:T(8,128)(2,1)S(1)} %fusion.26), channel_id=1, source_target_pairs={{2,0},{3,1},{4,2},{5,3},{6,4},{7,5},{8,6},{9,7},{10,8},{11,9},{12,... | collective-permute-start | bytes 491528 | tf_op jit(solution)/shard_map/ppermute | solution.py:16
  228.4 25.2 %collective-permute-start.13 = (bf16[5,128,128]{2,0,1:T(8,128)(2,1)}, bf16[5,128,128]{2,0,1:T(8,128)(2,1)}, u32[]{:S(2)}, u32[]{:S(2)}) collective-permute-start(bf16[5,128,128]{2,0,1:T(8,128)(2,1)} %fusion.29), channel_id=1, source_target_pairs={{1,0},{2,1},{3,2},{4,3},{5,4},{6,5},{7,6},{8,7},{9,8},{10,9},{11,1... | collective-permute-start | bytes 491528 | tf_op jit(solution)/shard_map/ppermute | solution.py:16
  235.1 18.5 %collective-permute-start.14 = (bf16[5,128,128]{2,0,1:T(8,128)(2,1)}, bf16[5,128,128]{2,0,1:T(8,128)(2,1)}, u32[]{:S(2)}, u32[]{:S(2)}) collective-permute-start(bf16[5,128,128]{2,0,1:T(8,128)(2,1)} %fusion.32), channel_id=1, source_target_pairs={{0,1},{1,2},{2,3},{3,4},{4,5},{5,6},{6,7},{7,8},{8,9},{9,10},{10,1... | collective-permute-start | bytes 491528 | tf_op jit(solution)/shard_map/ppermute | solution.py:16
  241.2 12.4 %collective-permute-start.15 = (bf16[5,128,128]{2,0,1:T(8,128)(2,1)}, bf16[5,128,128]{2,0,1:T(8,128)(2,1)}, u32[]{:S(2)}, u32[]{:S(2)}) collective-permute-start(bf16[5,128,128]{2,0,1:T(8,128)(2,1)} %fusion.35), channel_id=1, source_target_pairs={{0,2},{1,3},{2,4},{3,5},{4,6},{5,7},{6,8},{7,9},{8,10},{9,11},{10,... | collective-permute-start | bytes 491528 | tf_op jit(solution)/shard_map/ppermute | solution.py:16
  246.7 14.5 %collective-permute-start.16 = (bf16[5,128,128]{2,0,1:T(8,128)(2,1)}, bf16[5,128,128]{2,0,1:T(8,128)(2,1)}, u32[]{:S(2)}, u32[]{:S(2)}) collective-permute-start(bf16[5,128,128]{2,0,1:T(8,128)(2,1)} %fusion.38), channel_id=1, source_target_pairs={{0,3},{1,4},{2,5},{3,6},{4,7},{5,8},{6,9},{7,10},{8,11},{9,12},{10... | collective-permute-start | bytes 491528 | tf_op jit(solution)/shard_map/ppermute | solution.py:16
  251.7 15.7 %collective-permute-start.17 = (bf16[5,128,128]{2,0,1:T(8,128)(2,1)}, bf16[5,128,128]{2,0,1:T(8,128)(2,1)}, u32[]{:S(2)}, u32[]{:S(2)}) collective-permute-start(bf16[5,128,128]{2,0,1:T(8,128)(2,1)} %fusion.41), channel_id=1, source_target_pairs={{0,4},{1,5},{2,6},{3,7},{4,8},{5,9},{6,10},{7,11},{8,12},{9,13},{1... | collective-permute-start | bytes 491528 | tf_op jit(solution)/shard_map/ppermute | solution.py:16
Sparse Core Ops, SparseCore 0:
  66.4 137.6 all-reduce.2
where the time goes:
time: 279 us; the launch traced here: 277 us
  waiting for transfers between devices  153 us (55%)
  starting transfers between devices  63.2 us (23%)
  matrix products  23.8 us (9%)
  local copies, waits for them, and re-layouts  20.1 us (7%)
  between operations  13.8 us (5%)
  other arithmetic  3.73 us (1%)
    psum x1, waiting for transfers between devices, shards(): lax.psum(partial_value.astype(jnp.bfloat16), 'coef').astype(jnp.float32)  136 us
    ppermute x16, starting transfers between devices, from_behind(): return lax.ppermute(block, axis, route)  55.9 us
    dot_general x9, matrix products, shards(): contribs[offset] = jnp.einsum('js,sro->jro', select, tiles)  14.4 us
    ppermute x16, waiting for transfers between devices, from_behind(): return lax.ppermute(block, axis, route)  13.8 us
    unnamed x22, local copies, waits for them, and re-layouts  11.6 us
    dot_general x1, matrix products, shards(): lax.dot_general(basis_values, weighted, (((0,), (0,)), ((), ())), preferr...  5.96 us
  transfers between devices with their start and end apart: 19, of which 5 were waited for; matrix products, arithmetic and copies ran while one was open for 9% of the time, Pallas kernels for 0%

commit v1 on v0

--- a/solution.py
+++ b/solution.py
@@ -8,6 +8,12 @@
 PANELS_DEV = 5
 REACH = 4
 LISTED = 21
+
+
+def add_all(array, axis):
+    parts = lax.all_gather(array, axis, axis=0, tiled=False)
+    summed = parts.sum(axis=0)
+    return summed
 
 
 def from_behind(block, axis, distance):
@@ -57,7 +63,7 @@
         field, near, (((1,), (1,)), ((), ())), preferred_element_type=jnp.float32
     )
     partial_value = partial_value / jnp.sqrt(jnp.float32(ORBITALS))
-    density = lax.psum(partial_value.astype(jnp.bfloat16), "coef").astype(jnp.float32)
+    density = add_all(partial_value.astype(jnp.bfloat16), "coef").astype(jnp.float32)
     anchor = jnp.zeros((), jnp.int32)
     start = batch * points
     padded_centres = jnp.pad(centres, ((0, 0), (points, points)))

time: 279 us -> 545 us (1.95)
  the two profiles are of different devices: /device:TPU:388 before, /device:TPU:390 now
where the time goes in v1:
time: 545 us; the launch traced here: 544 us
  waiting for transfers between devices  406 us (74%)
  starting transfers between devices  64 us (12%)
  matrix products  23.8 us (4%)
  local copies, waits for them, and re-layouts  20.1 us (4%)
  other arithmetic  16.1 us (3%)
  between operations  13.7 us (3%)
    all_gather x1, waiting for transfers between devices, add_all(): parts = lax.all_gather(array, axis, axis=0, tiled=False)  389 us
    ppermute x16, starting transfers between devices, from_behind(): return lax.ppermute(block, axis, route)  56.8 us
    dot_general x9, matrix products, shards(): contribs[offset] = jnp.einsum('js,sro->jro', select, tiles)  14.4 us
    ppermute x16, waiting for transfers between devices, from_behind(): return lax.ppermute(block, axis, route)  13.8 us
    reduce_sum x1, other arithmetic, add_all(): summed = parts.sum(axis=0)  12.4 us
    unnamed x22, local copies, waits for them, and re-layouts  11.6 us
  transfers between devices with their start and end apart: 19, of which 5 were waited for; matrix products, arithmetic and copies ran while one was open for 4% of the time, Pallas kernels for 0%

profile of v1, /device:TPU:390, one launch (start us, length us, event | category | flops | bytes accessed | tf_op | source)
XLA Modules:
  0.0 543.8 jit_solution(5728147668214267611)
XLA Ops:
  6.5 3.2 collective-permute-start
  9.7 2.9 collective-permute-start.1
  12.7 4.0 collective-permute-start.2
  16.7 1.9 collective-permute-start.3
  18.6 5.1 collective-permute-start.4
  25.2 5.4 collective-permute-start.5
  30.7 1.6 constant_dynamic-update-slice_fusion.8
  32.2 1.9 collective-permute-start.6
  34.2 1.6 constant_dynamic-update-slice_fusion.7
  35.7 2.9 collective-permute-start.7
  38.7 1.6 constant_dynamic-update-slice_fusion.6
  40.3 1.6 constant_dynamic-update-slice_fusion.5
  41.8 1.6 constant_dynamic-update-slice_fusion.4
  43.4 1.6 constant_dynamic-update-slice_fusion.3
  47.1 2.9 gather_fusion
  50.0 2.4 bitcast_select_fusion
  52.3 1.1 convolution_convert_fusion
  53.5 3.4 collective-permute-start.8
  56.9 3.8 collective-permute-start.9
  60.7 1.1 collective-permute-done.8
  61.8 1.8 collective-permute-done.9
  64.2 2.3 multiply_convert_fusion.1
  66.6 0.9 dynamic-slice_reduce_fusion.2
  67.5 1.0 fusion.49
  68.6 389.4 %all-gather.3.cloned.1.call-done = bf16[5120,1920]{1,0:T(8,128)(2,1)} async-done(((bf16[640,1920]{1,0:T(8,128)(2,1)}), bf16[5120,1920]{1,0:T(8,128)(2,1)}) %all-gather.3.cloned.1.call-update) | async-done | bytes 19660816 | tf_op jit(solution)/shard_map/all_gather | solution.py:14
  458.0 12.4 %reduce_sum.12 = bf16[640,1920]{1,0:T(8,128)(2,1)} reduce(bf16[8,640,1920]{2,1,0:T(8,128)(2,1)} %bitcast.59, bf16[]{:T(256)} %constant.22.clone.1), dimensions={0}, to_apply=%region_0.1 | reduce | flops 8601600 | bytes 22118402 | tf_op jit(solution)/shard_map/reduce_sum | solution.py:15
  470.3 6.0 %fusion = bf16[2688,128]{0,1:T(8,128)(2,1)} fusion(bf16[640,2688]{1,0:T(8,128)(2,1)S(1)} %copy-done, bf16[640,1920]{1,0:T(8,128)(2,1)} %reduce_sum.12, f32[1920]{0:T(1024)S(1)} %get-tuple-element.10, f32[640]{0:T(1024)S(1)} %get-tuple-element.7, f32[1920]{0:T(1024)S(1)} %get-tuple-element.9, f32[640]{0:T(1024)S(1)} %get-tuple-element.6, ...), kind=kOutput, calls=%fused_computation.4 | convolution fusion | flops 772128768 | bytes 7111168 | tf_op jit(solution)/shard_map/dot_general | solution.py:82
  476.3 2.2 copy.15
  478.5 1.8 fusion.20
  480.3 4.5 collective-permute-start.10
  484.8 1.7 fusion.23
  486.6 2.4 collective-permute-start.11
  489.0 1.7 fusion.26
  490.7 3.1 collective-permute-start.12
  493.8 1.4 fusion.29
  495.2 5.1 collective-permute-start.13
  500.3 1.3 fusion.32
  501.6 2.1 collective-permute-start.14
  503.7 1.3 fusion.35
  505.1 1.3 fusion.38
  506.4 1.3 fusion.41
  507.8 5.2 collective-permute-start.15
  512.9 5.0 collective-permute-start.16
  517.9 1.9 collective-permute-start.17
  519.9 7.7 %collective-permute-done.16 = bf16[5,128,128]{2,0,1:T(8,128)(2,1)} collective-permute-done((bf16[5,128,128]{2,0,1:T(8,128)(2,1)}, bf16[5,128,128]{2,0,1:T(8,128)(2,1)}, u32[]{:S(2)}, u32[]{:S(2)}) %collective-permute-start.16) | collective-permute-done | bytes 163872 | tf_op jit(solution)/shard_map/ppermute | solution.py:22
  527.6 6.1 %collective-permute-done.17 = bf16[5,128,128]{2,0,1:T(8,128)(2,1)} collective-permute-done((bf16[5,128,128]{2,0,1:T(8,128)(2,1)}, bf16[5,128,128]{2,0,1:T(8,128)(2,1)}, u32[]{:S(2)}, u32[]{:S(2)}) %collective-permute-start.17) | collective-permute-done | bytes 163872 | tf_op jit(solution)/shard_map/ppermute | solution.py:22
  533.7 2.5 convert_add_fusion
  536.2 0.8 copy.25
  (46 shorter events, 4.2 us)
Async XLA Ops:
  6.5 45.8 %copy-start = (bf16[640,2688]{1,0:T(8,128)(2,1)S(1)}, bf16[640,2688]{1,0:T(8,128)(2,1)}, u32[]{:S(2)}) copy-start(bf16[640,2688]{1,0:T(8,128)(2,1)} %param.5) | copy-start | bytes 10321924
  6.5 451.4 %all-gather.3.cloned.1.call-start = ((), (), s32[]{:S(2)}) async-start(), calls=%async_computation | async-start | bytes 22118400 | tf_op jit(solution)/shard_map/all_gather | solution.py:14
  6.5 18.7 %collective-permute-start = (bf16[5,128,128]{2,1,0:T(8,128)(2,1)}, bf16[5,128,128]{2,1,0:T(8,128)(2,1)}, u32[]{:S(2)}, u32[]{:S(2)}) collective-permute-start(bf16[5,128,128]{2,1,0:T(8,128)(2,1)} %bitcast.64), channel_id=1, source_target_pairs={{0,4},{1,5},{2,6},{3,7},{4,8},{5,9},{6,10},{7,11},{8,12},{9,13},{1... | collective-permute-start | bytes 491528 | tf_op jit(solution)/shard_map/ppermute | solution.py:22
  9.7 22.5 %collective-permute-start.1 = (bf16[5,128,128]{2,1,0:T(8,128)(2,1)}, bf16[5,128,128]{2,1,0:T(8,128)(2,1)}, u32[]{:S(2)}, u32[]{:S(2)}) collective-permute-start(bf16[5,128,128]{2,1,0:T(8,128)(2,1)} %bitcast.65), channel_id=1, source_target_pairs={{0,3},{1,4},{2,5},{3,6},{4,7},{5,8},{6,9},{7,10},{8,11},{9,12},{10... | collective-permute-start | bytes 491528 | tf_op jit(solution)/shard_map/ppermute | solution.py:22
  12.7 23.1 %collective-permute-start.2 = (bf16[5,128,128]{2,1,0:T(8,128)(2,1)}, bf16[5,128,128]{2,1,0:T(8,128)(2,1)}, u32[]{:S(2)}, u32[]{:S(2)}) collective-permute-start(bf16[5,128,128]{2,1,0:T(8,128)(2,1)} %bitcast.66), channel_id=1, source_target_pairs={{0,2},{1,3},{2,4},{3,5},{4,6},{5,7},{6,8},{7,9},{8,10},{9,11},{10,... | collective-permute-start | bytes 491528 | tf_op jit(solution)/shard_map/ppermute | solution.py:22
  16.7 23.5 %collective-permute-start.3 = (bf16[5,128,128]{2,1,0:T(8,128)(2,1)}, bf16[5,128,128]{2,1,0:T(8,128)(2,1)}, u32[]{:S(2)}, u32[]{:S(2)}) collective-permute-start(bf16[5,128,128]{2,1,0:T(8,128)(2,1)} %bitcast.67), channel_id=1, source_target_pairs={{0,1},{1,2},{2,3},{3,4},{4,5},{5,6},{6,7},{7,8},{8,9},{9,10},{10,1... | collective-permute-start | bytes 491528 | tf_op jit(solution)/shard_map/ppermute | solution.py:22
  18.6 24.8 %collective-permute-start.4 = (bf16[5,128,128]{2,1,0:T(8,128)(2,1)}, bf16[5,128,128]{2,1,0:T(8,128)(2,1)}, u32[]{:S(2)}, u32[]{:S(2)}) collective-permute-start(bf16[5,128,128]{2,1,0:T(8,128)(2,1)} %bitcast.68), channel_id=1, source_target_pairs={{1,0},{2,1},{3,2},{4,3},{5,4},{6,5},{7,6},{8,7},{9,8},{10,9},{11,1... | collective-permute-start | bytes 491528 | tf_op jit(solution)/shard_map/ppermute | solution.py:22
  25.2 19.8 %collective-permute-start.5 = (bf16[5,128,128]{2,1,0:T(8,128)(2,1)}, bf16[5,128,128]{2,1,0:T(8,128)(2,1)S(1)}, u32[]{:S(2)}, u32[]{:S(2)}) collective-permute-start(bf16[5,128,128]{2,1,0:T(8,128)(2,1)} %bitcast.69), channel_id=1, source_target_pairs={{2,0},{3,1},{4,2},{5,3},{6,4},{7,5},{8,6},{9,7},{10,8},{11,9},{12,... | collective-permute-start | bytes 491528 | tf_op jit(solution)/shard_map/ppermute | solution.py:22
  32.2 13.5 %collective-permute-start.6 = (bf16[5,128,128]{2,1,0:T(8,128)(2,1)}, bf16[5,128,128]{2,1,0:T(8,128)(2,1)S(1)}, u32[]{:S(2)}, u32[]{:S(2)}) collective-permute-start(bf16[5,128,128]{2,1,0:T(8,128)(2,1)} %bitcast.70), channel_id=1, source_target_pairs={{3,0},{4,1},{5,2},{6,3},{7,4},{8,5},{9,6},{10,7},{11,8},{12,9},{13... | collective-permute-start | bytes 491528 | tf_op jit(solution)/shard_map/ppermute | solution.py:22
  35.7 10.6 %collective-permute-start.7 = (bf16[5,128,128]{2,1,0:T(8,128)(2,1)}, bf16[5,128,128]{2,1,0:T(8,128)(2,1)S(1)}, u32[]{:S(2)}, u32[]{:S(2)}) collective-permute-start(bf16[5,128,128]{2,1,0:T(8,128)(2,1)} %bitcast.71), channel_id=1, source_target_pairs={{4,0},{5,1},{6,2},{7,3},{8,4},{9,5},{10,6},{11,7},{12,8},{13,9},{1... | collective-permute-start | bytes 491528 | tf_op jit(solution)/shard_map/ppermute | solution.py:22
  53.5 10.1 %copy-start.2 = (bf16[128,640]{1,0:T(8,128)(2,1)}, bf16[128,640]{1,0:T(8,128)(2,1)S(1)}, u32[]{:S(2)}) copy-start(bf16[128,640]{1,0:T(8,128)(2,1)S(1)} %convolution_convert_fusion) | copy-start | bytes 491524
  53.5 8.3 %collective-permute-start.8 = (bf16[640,128]{0,1:T(8,128)(2,1)S(1)}, bf16[640,128]{0,1:T(8,128)(2,1)S(1)}, u32[]{:S(2)}, u32[]{:S(2)}) collective-permute-start(bf16[640,128]{0,1:T(8,128)(2,1)S(1)} %bitcast.60), channel_id=1, source_target_pairs={{0,1},{1,2},{2,3},{3,4},{4,5},{5,6},{6,7},{7,8},{8,9},{9,10},{10,1... | collective-permute-start | bytes 491528 | tf_op jit(solution)/shard_map/ppermute | solution.py:30
  56.9 6.7 %collective-permute-start.9 = (bf16[640,128]{0,1:T(8,128)(2,1)S(1)}, bf16[640,128]{0,1:T(8,128)(2,1)S(1)}, u32[]{:S(2)}, u32[]{:S(2)}) collective-permute-start(bf16[640,128]{0,1:T(8,128)(2,1)S(1)} %bitcast.61), channel_id=1, source_target_pairs={{1,0},{2,1},{3,2},{4,3},{5,4},{6,5},{7,6},{8,7},{9,8},{10,9},{11,1... | collective-permute-start | bytes 491528 | tf_op jit(solution)/shard_map/ppermute | solution.py:33
  61.8 1.8 copy-start.3
  63.6 0.7 copy-start.4
  458.0 12.4 %copy-start.6 = (f32[640]{0:T(1024)S(1)}, f32[640]{0:T(1024)}, u32[]{:S(2)}) copy-start(f32[640]{0:T(1024)} %param.9) | copy-start | bytes 7684
  470.3 8.2 %copy-start.5 = (s32[1,21]{1,0:T(1,128)S(1)}, s32[1,21]{1,0:T(1,128)}, u32[]{:S(2)}) copy-start(s32[1,21]{1,0:T(1,128)} %param.7) | copy-start | bytes 256
  478.5 15.3 %copy-start.1 = (bf16[2688,128]{1,0:T(8,128)(2,1)S(1)}, bf16[2688,128]{1,0:T(8,128)(2,1)}, u32[]{:S(2)}) copy-start(bf16[2688,128]{1,0:T(8,128)(2,1)} %copy.15) | copy-start | bytes 2064388
  480.3 27.4 %collective-permute-start.10 = (bf16[5,128,128]{2,0,1:T(8,128)(2,1)S(1)}, bf16[5,128,128]{2,0,1:T(8,128)(2,1)}, u32[]{:S(2)}, u32[]{:S(2)}) collective-permute-start(bf16[5,128,128]{2,0,1:T(8,128)(2,1)S(1)} %fusion.20), channel_id=1, source_target_pairs={{4,0},{5,1},{6,2},{7,3},{8,4},{9,5},{10,6},{11,7},{12,8},{13,9},{1... | collective-permute-start | bytes 491528 | tf_op jit(solution)/shard_map/ppermute | solution.py:22
  486.6 26.4 %collective-permute-start.11 = (bf16[5,128,128]{2,0,1:T(8,128)(2,1)S(1)}, bf16[5,128,128]{2,0,1:T(8,128)(2,1)}, u32[]{:S(2)}, u32[]{:S(2)}) collective-permute-start(bf16[5,128,128]{2,0,1:T(8,128)(2,1)S(1)} %fusion.23), channel_id=1, source_target_pairs={{3,0},{4,1},{5,2},{6,3},{7,4},{8,5},{9,6},{10,7},{11,8},{12,9},{13... | collective-permute-start | bytes 491528 | tf_op jit(solution)/shard_map/ppermute | solution.py:22
  490.7 27.2 %collective-permute-start.12 = (bf16[5,128,128]{2,0,1:T(8,128)(2,1)S(1)}, bf16[5,128,128]{2,0,1:T(8,128)(2,1)}, u32[]{:S(2)}, u32[]{:S(2)}) collective-permute-start(bf16[5,128,128]{2,0,1:T(8,128)(2,1)S(1)} %fusion.26), channel_id=1, source_target_pairs={{2,0},{3,1},{4,2},{5,3},{6,4},{7,5},{8,6},{9,7},{10,8},{11,9},{12,... | collective-permute-start | bytes 491528 | tf_op jit(solution)/shard_map/ppermute | solution.py:22
  495.2 24.7 %collective-permute-start.13 = (bf16[5,128,128]{2,0,1:T(8,128)(2,1)}, bf16[5,128,128]{2,0,1:T(8,128)(2,1)}, u32[]{:S(2)}, u32[]{:S(2)}) collective-permute-start(bf16[5,128,128]{2,0,1:T(8,128)(2,1)} %fusion.29), channel_id=1, source_target_pairs={{1,0},{2,1},{3,2},{4,3},{5,4},{6,5},{7,6},{8,7},{9,8},{10,9},{11,1... | collective-permute-start | bytes 491528 | tf_op jit(solution)/shard_map/ppermute | solution.py:22
  501.6 18.2 %collective-permute-start.14 = (bf16[5,128,128]{2,0,1:T(8,128)(2,1)}, bf16[5,128,128]{2,0,1:T(8,128)(2,1)}, u32[]{:S(2)}, u32[]{:S(2)}) collective-permute-start(bf16[5,128,128]{2,0,1:T(8,128)(2,1)} %fusion.32), channel_id=1, source_target_pairs={{0,1},{1,2},{2,3},{3,4},{4,5},{5,6},{6,7},{7,8},{8,9},{9,10},{10,1... | collective-permute-start | bytes 491528 | tf_op jit(solution)/shard_map/ppermute | solution.py:22
  507.8 12.1 %collective-permute-start.15 = (bf16[5,128,128]{2,0,1:T(8,128)(2,1)}, bf16[5,128,128]{2,0,1:T(8,128)(2,1)}, u32[]{:S(2)}, u32[]{:S(2)}) collective-permute-start(bf16[5,128,128]{2,0,1:T(8,128)(2,1)} %fusion.35), channel_id=1, source_target_pairs={{0,2},{1,3},{2,4},{3,5},{4,6},{5,7},{6,8},{7,9},{8,10},{9,11},{10,... | collective-permute-start | bytes 491528 | tf_op jit(solution)/shard_map/ppermute | solution.py:22
  512.9 14.7 %collective-permute-start.16 = (bf16[5,128,128]{2,0,1:T(8,128)(2,1)}, bf16[5,128,128]{2,0,1:T(8,128)(2,1)}, u32[]{:S(2)}, u32[]{:S(2)}) collective-permute-start(bf16[5,128,128]{2,0,1:T(8,128)(2,1)} %fusion.38), channel_id=1, source_target_pairs={{0,3},{1,4},{2,5},{3,6},{4,7},{5,8},{6,9},{7,10},{8,11},{9,12},{10... | collective-permute-start | bytes 491528 | tf_op jit(solution)/shard_map/ppermute | solution.py:22
  517.9 15.8 %collective-permute-start.17 = (bf16[5,128,128]{2,0,1:T(8,128)(2,1)}, bf16[5,128,128]{2,0,1:T(8,128)(2,1)}, u32[]{:S(2)}, u32[]{:S(2)}) collective-permute-start(bf16[5,128,128]{2,0,1:T(8,128)(2,1)} %fusion.41), channel_id=1, source_target_pairs={{0,4},{1,5},{2,6},{3,7},{4,8},{5,9},{6,10},{7,11},{8,12},{9,13},{1... | collective-permute-start | bytes 491528 | tf_op jit(solution)/shard_map/ppermute | solution.py:22
Sparse Core Ops, SparseCore 0:
  66.7 391.2 all-gather.2
